TPU v7x, 32 devices: a whole 2x2x4 slice. The times are simulated.
32 devices in a mesh: mp: 4 (over y, x), dp: 8 (over z, core).
Axes of the slice: x: 2, y: 2, z: 4, core: 2. Of those that a mesh axis runs over, the one named last changes fastest.
Arguments:
- inputs: bfloat16 [1280, 8192], P('dp'), may hold values from -60 to 60
- cotangent: bfloat16 [1280, 16384], P('dp', 'mp'), may hold values from -11 to 11
- weight: float32 [8192, 16384], P('dp', 'mp'), may hold values from -6 to 6
- row_moment: float32 [8192], P('dp'), may hold values from 0.05 to 0.5
- col_moment: float32 [16384], P('mp'), may hold values from 0.01 to 60
Outputs:
- new_weight: float32 [8192, 16384], P('dp', 'mp')
- update: bfloat16 [8192, 16384], P('dp', 'mp')
- new_rows: float32 [8192], P('dp')
- new_cols: float32 [16384], P('mp')
All inputs are finite; a program needn't handle non-finite values.
Results may differ from a plain program's by a relative error of at most 0.001.
Values may be sent and summed in bfloat16 or wider, within the bound.
A program may use at most 128 MiB of HBM per device.

v0:
```python
import jax
import jax.numpy as jnp
from jax import lax
from jax.sharding import PartitionSpec as P

D = 8192
F = 16384


decay_rate = 1.0 - 10.0 ** (-0.8)
step_size = 0.05
tiny_eps = 1e-30


def contract(left, right):
    return lax.dot_general(
        left, right, (((0,), (0,)), ((), ())), preferred_element_type=jnp.float32
    )


def on_device(inputs, cotangent, weight, row_moment, col_moment):
    feat_rows = lax.all_to_all(inputs, "dp", split_axis=1, concat_axis=0, tiled=True)
    gradient = contract(feat_rows, lax.all_gather(cotangent, "dp", axis=0, tiled=True))
    squares = gradient * gradient + tiny_eps
    row_part = jnp.sum(squares, axis=1)
    col_part = jnp.sum(squares, axis=0)
    weight_sq = jnp.sum(weight * weight)
    row_total, weight_mp = lax.psum((row_part, weight_sq), "mp")
    new_rows = decay_rate * row_moment + (1.0 - decay_rate) * (row_total / F)
    col_total, rows_sum, weight_all = lax.psum((col_part, jnp.sum(new_rows), weight_mp), "dp")
    new_cols = decay_rate * col_moment + (1.0 - decay_rate) * (col_total / D)
    row_mean = rows_sum / D
    scaled = gradient / jnp.sqrt(new_rows[:, None] * new_cols[None, :] / row_mean)
    scaled_sq = lax.psum(jnp.sum(scaled * scaled), ("mp", "dp"))
    update_rms = jnp.sqrt(scaled_sq / (D * F))
    clipped = scaled / jnp.maximum(1.0, update_rms)
    weight_rms = jnp.sqrt(weight_all / (D * F))
    new_weight = weight - step_size * weight_rms * clipped
    return (new_weight, clipped.astype(jnp.bfloat16), new_rows, new_cols)


def solution(mesh):
    return jax.shard_map(
        on_device,
        mesh=mesh,
        in_specs=(P("dp", None), P("dp", "mp"), P("dp", "mp"), P("dp"), P("mp")),
        out_specs=(P("dp", "mp"), P("dp", "mp"), P("dp"), P("mp")),
        check_vma=False,
    )
```

profile of v0, /device:TPU:0, one launch (start us, length us, event | category | flops | bytes accessed | tf_op | source)
XLA Modules:
  0.0 295.3 jit_solution(7954267839116123947)
XLA Ops:
  7.2 0.0 all-gather.2.cloned.1.call-start
  7.2 0.7 all-gather.2.cloned.1.call-update
  7.9 3.6 %copy.13 = bf16[20,8,8,1024]{3,2,0,1:T(8,128)(2,1)} copy(bf16[20,8,8,1024]{3,2,1,0:T(8,128)(2,1)} %bitcast.9) | data formatting | bytes 5242880 | tf_op jit(solution)/shard_map/all_to_all | solution.py:22
  11.5 6.3 %all-to-all-start = ((bf16[160,8,1024]{2,0,1:T(8,128)(2,1)}), bf16[160,8,1024]{2,0,1:T(8,128)(2,1)S(1)}, u32[]{:S(2)}, u32[]{:S(2)}) async-start(bf16[160,8,1024]{2,0,1:T(8,128)(2,1)} %bitcast.8), calls=%async_computation | async-start | bytes 5242880 | tf_op jit(solution)/shard_map/all_to_all | solution.py:22
  17.8 12.4 %multiply_reduce_fusion.1 = f32[]{:T(128)} fusion(f32[1024,4096]{1,0:T(8,128)} %param.7), kind=kLoop, calls=%fused_computation.4 | loop fusion | flops 8388607 | bytes 16777220 | tf_op jit(solution)/shard_map/reduce_sum | solution.py:27
  30.2 116.5 %all-to-all-done = bf16[160,8,1024]{2,0,1:T(8,128)(2,1)S(1)} async-done(((bf16[160,8,1024]{2,0,1:T(8,128)(2,1)}), bf16[160,8,1024]{2,0,1:T(8,128)(2,1)S(1)}, u32[]{:S(2)}, u32[]{:S(2)}) %all-to-all-start) | async-done | bytes 2621472 | tf_op jit(solution)/shard_map/all_to_all | solution.py:22
  146.7 17.3 %all-gather.2.cloned.1.call-done = bf16[1280,4096]{1,0:T(8,128)(2,1)} async-done(((bf16[160,4096]{1,0:T(8,128)(2,1)}), bf16[1280,4096]{1,0:T(8,128)(2,1)}) %all-gather.2.cloned.1.call-update) | async-done | bytes 10485776 | tf_op jit(solution)/shard_map/all_gather | solution.py:23
  164.1 0.0 copy-start.3
  164.1 0.0 copy-start.2
  164.1 18.7 %fusion = (f32[4096]{0:T(1024)S(1)}, f32[1024]{0:T(1024)S(1)}, f32[1024,4096]{1,0:T(8,128)}) fusion(bf16[1280,1024]{1,0:T(8,128)(2,1)S(1)} %bitcast.10, bf16[1280,4096]{1,0:T(8,128)(2,1)} %all-gather.2.cloned.1.call-done), kind=kOutput, calls=%fused_computation.5 | convolution fusion | flops 10754190336 | bytes 29904896 | tf_op jit(solution)/shard_map/dot_general | solution.py:16
  182.8 10.7 %all-reduce.1 = (f32[]{:T(128)}, f32[1024]{0:T(1024)S(1)}) all-reduce(f32[]{:T(128)} %multiply_reduce_fusion.1, f32[1024]{0:T(1024)S(1)} %get-tuple-element.5), channel_id=1, replica_groups=mesh['mp'=4,'dp'=8] {'mp'}, use_global_device_ids=true, to_apply=%region_1.0 | all-reduce | flops 1025 | bytes 8200 | tf_op jit(solution)/shard_map/psum | solution.py:28
  193.4 0.0 copy-done.3
  193.4 0.6 fusion.3
  194.0 0.0 copy-start.1
  194.0 27.0 %all-reduce = (f32[]{:T(128)}, f32[]{:T(128)}, f32[4096]{0:T(1024)S(1)}) all-reduce(f32[]{:T(128)} %get-tuple-element.9, f32[]{:T(128)} %get-tuple-element.11, f32[4096]{0:T(1024)S(1)} %get-tuple-element.4), channel_id=1, replica_groups=mesh['mp'=4,'dp'=8] {'dp'}, use_global_device_ids=true, to_apply=%region_2.0 | all-reduce | flops 4098 | bytes 32784 | tf_op jit(solution)/shard_map/psum | solution.py:30
  222.3 0.0 copy-done.2
  222.4 0.0 copy-start
  222.4 9.0 %multiply_reduce_fusion = f32[]{:T(128)} fusion(f32[1024,4096]{1,0:T(8,128)} %get-tuple-element.15, f32[]{:T(128)S(6)} %div.29, f32[4096]{0:T(1024)S(1)} %multiply_add_fusion.1, f32[1024]{0:T(1024)S(1)} %get-tuple-element.12), kind=kLoop, calls=%fused_computation.1 | loop fusion | flops 20971520 | bytes 16797704 | tf_op jit(solution)/shard_map/reduce_sum | solution.py:34
  231.4 37.1 %psum.47 = f32[]{:T(128)} all-reduce(f32[]{:T(128)} %multiply_reduce_fusion), channel_id=1, replica_groups=mesh['mp'=4,'dp'=8] {'mp','dp'}, use_global_device_ids=true, to_apply=%region_10.0 | all-reduce | flops 1 | bytes 8 | tf_op jit(solution)/shard_map/psum | solution.py:34
  269.2 19.3 %fusion.2 = (bf16[1024,4096]{1,0:T(8,128)(2,1)}, f32[1024,4096]{1,0:T(8,128)}) fusion(f32[]{:T(128)S(6)} %max_shard_map.3, f32[1024,4096]{1,0:T(8,128)} %get-tuple-element.15, f32[]{:T(128)S(6)} %div.29, f32[4096]{0:T(1024)S(1)} %multiply_add_fusion.1, f32[1024]{0:T(1024)S(1)} %get-tuple-element.12, f32[1024,4096]{1,0:T(8,128)} %param.7, f32[]{:T(128)S(6)} %mul_shard_map.3), kind=kLoop, calls=%fused_computation.8 | loop fusion | flops 29360128 | bytes 58740748 | tf_op jit(solution)/shard_map/convert_element_type | solution.py:39
  288.4 0.0 copy-done.1
  288.4 0.0 copy-done
  (1 shorter events, 0.0 us)
Async XLA Ops:
  7.2 156.9 %all-gather.2.cloned.1.call-start = ((), (), s32[]{:S(2)}) async-start(), calls=%async_computation.1 | async-start | bytes 11796480 | tf_op jit(solution)/shard_map/all_gather | solution.py:23
  11.5 135.3 %all-to-all-start = ((bf16[160,8,1024]{2,0,1:T(8,128)(2,1)}), bf16[160,8,1024]{2,0,1:T(8,128)(2,1)S(1)}, u32[]{:S(2)}, u32[]{:S(2)}) async-start(bf16[160,8,1024]{2,0,1:T(8,128)(2,1)} %bitcast.8), calls=%async_computation | async-start | bytes 5242880 | tf_op jit(solution)/shard_map/all_to_all | solution.py:22
  164.1 29.4 %copy-start.3 = (f32[1024]{0:T(1024)S(1)}, f32[1024]{0:T(1024)}, u32[]{:S(2)}) copy-start(f32[1024]{0:T(1024)} %param.8) | copy-start | bytes 12292
  164.1 58.3 %copy-start.2 = (f32[4096]{0:T(1024)S(1)}, f32[4096]{0:T(1024)}, u32[]{:S(2)}) copy-start(f32[4096]{0:T(1024)} %param.9) | copy-start | bytes 49156
  194.0 94.4 %copy-start.1 = (f32[1024]{0:T(1024)}, f32[1024]{0:T(1024)S(1)}, u32[]{:S(2)}) copy-start(f32[1024]{0:T(1024)S(1)} %get-tuple-element.12) | copy-start | bytes 12292
  222.4 66.1 %copy-start = (f32[4096]{0:T(1024)}, f32[4096]{0:T(1024)S(1)}, u32[]{:S(2)}) copy-start(f32[4096]{0:T(1024)S(1)} %multiply_add_fusion.1) | copy-start | bytes 49156
Sparse Core Ops, SparseCore 0:
  9.6 154.3 all-gather.1
where the time goes:
time: 297 us; the launch traced here: 295 us
  waiting for transfers between devices  135 us (45%)
  blocking collectives  74.8 us (25%)
  other arithmetic  41.3 us (14%)
  matrix products  18.7 us (6%)
  between operations  16.1 us (5%)
  starting transfers between devices  6.36 us (2%)
  local copies, waits for them, and re-layouts  3.59 us (1%)
    all_to_all x1, waiting for transfers between devices, on_device(): lax.all_to_all(inputs, 'dp', split_axis=1, concat_axis=0, tiled=True)  117 us
    psum x1, blocking collectives, on_device(): scaled_sq = lax.psum(jnp.sum(scaled * scaled), ('mp', 'dp'))  37.1 us
    psum x1, blocking collectives, on_device(): lax.psum((col_part, jnp.sum(new_rows), weight_mp), 'dp')  27 us
    convert_element_type x1, other arithmetic, on_device(): return (new_weight, clipped.astype(jnp.bfloat16), new_rows, new_cols)  19.3 us
    dot_general x1, matrix products, contract(): lax.dot_general(left, right, (((0,), (0,)), ((), ())), preferred_element_...  18.7 us
    all_gather x1, waiting for transfers between devices, on_device(): lax.all_gather(cotangent, 'dp', axis=0, tiled=True)  17.3 us
    reduce_sum x1, other arithmetic, on_device(): weight_sq = jnp.sum(weight * weight)  12.4 us
    psum x1, blocking collectives, on_device(): row_total, weight_mp = lax.psum((row_part, weight_sq), 'mp')  10.7 us
  transfers between devices with their start and end apart: 2, of which 2 were waited for; matrix products, arithmetic and copies ran while one was open for 5% of the time, Pallas kernels for 0%

commit v1 on v0

v1 whole, which is shorter than its diff:
```python
import functools

import jax
import jax.numpy as jnp
from jax import lax
from jax.experimental import pallas as pl
from jax.experimental.pallas import tpu as pltpu
from jax.sharding import PartitionSpec as P

decay_rate = 1.0 - 10.0 ** (-0.8)
step_size = 0.05
tiny_eps = 1e-30

LANES = 128
MESH = pl.DeviceIdType.MESH
F32 = jnp.float32


def gather_kernel(
    MP, DP, W, BM,
    x_ref, cot_ref, w_ref, rm_ref, cm_ref,
    g_ref, nr_ref, nc_ref, rs_ref, cs_ref, sc_ref,
    a_raw, a_t, call, wbuf, row_acc, inv_r, inv_c, row_slots, col_slots, s_slots, t_slots,
    own_sem, wsem, in_send, in_recv, fwd_send, up_send, dn_send, sib_send,
    lane_recv, sib_recv, row_send, row_recv, col_send, col_recv,
    s_send, s_recv, t_send, t_recv,
):
    m = lax.axis_index("mp")
    me = lax.axis_index("dp")
    z, c = me // 2, me % 2
    Z = DP // 2
    sib = me + 1 - 2 * c
    T = x_ref.shape[0]
    R, C = g_ref.shape
    NC = C // W
    G = W // LANES
    D, F = R * DP, C * MP

    barrier = pltpu.get_barrier_semaphore()

    def greet_dp(q, _):
        pl.semaphore_signal(barrier, inc=1, device_id={"dp": (me + q) % DP}, device_id_type=MESH)
        return 0

    def greet_mp(q, _):
        pl.semaphore_signal(barrier, inc=1, device_id={"mp": (m + q) % MP}, device_id_type=MESH)
        return 0

    lax.fori_loop(1, DP, greet_dp, 0)
    lax.fori_loop(1, MP, greet_mp, 0)
    pl.semaphore_wait(barrier, DP + MP - 2)

    def rows_of(s):
        return pl.ds(pl.multiple_of(s * T, T), T)

    def cols_of(j):
        return pl.ds(pl.multiple_of(j * W, W), W)

    def feat_cols(d):
        return pl.ds(pl.multiple_of(d * R, R), R)

    def remote(src, dst, send, recv, **to):
        return pltpu.make_async_remote_copy(
            src_ref=src, dst_ref=dst, send_sem=send, recv_sem=recv,
            device_id=to, device_id_type=MESH,
        )

    def taker(s, d):
        return (s + (MP // 2) * (d % 2)) % MP

    def push(d):
        return remote(x_ref.at[:, feat_cols(d)], a_raw.at[rows_of(me), :],
                      in_send.at[d], in_recv.at[me], dp=d)

    def spread(s, q):
        return remote(a_raw.at[rows_of(s), :], a_raw.at[rows_of(s), :],
                      fwd_send.at[s, q], in_recv.at[s], mp=(m + q) % MP)

    def cot_block(zs, lane, j):
        return call.at[rows_of(zs * 2 + lane), cols_of(j)]

    def up(zs, j, src=None):
        dst = cot_block(zs, c, j)
        return remote(dst if src is None else src, dst, up_send.at[zs, j], lane_recv.at[zs, j], dp=(me + 2) % DP)

    def down(zs, j, src=None):
        dst = cot_block(zs, c, j)
        return remote(dst if src is None else src, dst, dn_send.at[zs, j], lane_recv.at[zs, j], dp=(me + DP - 2) % DP)

    def across(zs, j, src=None):
        dst = cot_block(zs, c, j)
        return remote(dst if src is None else src, dst, sib_send.at[zs, j], sib_recv.at[zs, j], dp=sib)

    def across_in(zs, j):
        dst = cot_block(zs, 1 - c, j)
        return remote(dst, dst, sib_send.at[zs, j], sib_recv.at[zs, j], dp=sib)

    own_x = pltpu.make_async_copy(x_ref.at[:, feat_cols(me)], a_raw.at[rows_of(me), :], own_sem.at[0])
    own_c = pltpu.make_async_copy(cot_ref, call.at[rows_of(me), :], own_sem.at[1])

    def push_step(d, _):
        @pl.when(jnp.logical_and(d != me, taker(me, d) == m))
        def _():
            push(d).start()
        return 0

    lax.fori_loop(0, DP, push_step, 0)
    own_x.start()
    own_c.start()

    def first_send(j, _):
        src = cot_ref.at[:, cols_of(j)]

        @pl.when(z < Z - 1)
        def _():
            up(z, j, src).start()

        @pl.when(z > 0)
        def _():
            down(z, j, src).start()

        across(z, j, src).start()
        return 0

    lax.fori_loop(0, NC, first_send, 0)

    WB = wbuf.shape[1]
    NW = R // WB

    def wcopy(i, slot):
        return pltpu.make_async_copy(w_ref.at[pl.ds(pl.multiple_of(i * WB, WB), WB), :], wbuf.at[slot], wsem.at[slot])

    wcopy(0, 0).start()

    def wstep(i, acc):
        slot = lax.rem(i, 2)

        @pl.when(i + 1 < NW)
        def _():
            wcopy(i + 1, 1 - slot).start()

        wcopy(i, slot).wait()

        def wcol(j, acc):
            v = wbuf[slot, :, cols_of(j)]
            return acc + jnp.sum((v * v).reshape(WB // 8, 8, W), axis=0)

        return lax.fori_loop(0, NC, wcol, acc)

    wacc = lax.fori_loop(0, NW, wstep, jnp.zeros((8, W), F32))
    wsq = sum(wacc[:, q * LANES:(q + 1) * LANES] for q in range(G))
    s_slots[m, 1] = wsq

    def take_step(s, _):
        @pl.when(jnp.logical_and(s != me, taker(s, me) == m))
        def _():
            spread(s, 1).wait_recv()

            def hand(q, _):
                spread(s, q).start()
                return 0

            lax.fori_loop(1, MP, hand, 0)
        return 0

    lax.fori_loop(0, DP, take_step, 0)

    def relay(k, j):
        lo, hi = z - k, z + k

        @pl.when(lo >= 0)
        def _():
            up(lo, j).wait_recv()

            @pl.when(z < Z - 1)
            def _():
                up(lo, j).start()

            across(lo, j).start()

        @pl.when(hi < Z)
        def _():
            down(hi, j).wait_recv()

            @pl.when(z > 0)
            def _():
                down(hi, j).start()

            across(hi, j).start()

    def relay_step(i, _):
        relay(1 + i // NC, i % NC)
        return 0

    lax.fori_loop(0, (Z - 2) * NC, relay_step, 0)

    def rest_step(s, _):
        @pl.when(jnp.logical_and(s != me, taker(s, me) != m))
        def _():
            spread(s, 1).wait_recv()
        return 0

    lax.fori_loop(0, DP, rest_step, 0)
    own_x.wait()
    own_c.wait()

    def turn(i, _):
        cols = pl.ds(pl.multiple_of(i * LANES, LANES), LANES)
        a_t[cols, :] = a_raw[:, cols].T
        return 0

    lax.fori_loop(0, R // LANES, turn, 0)
    row_acc[...] = jnp.zeros_like(row_acc)

    def chunk(j, _):
        relay(Z - 1, j)

        def sib_wait(zs, _):
            across_in(zs, j).wait_recv()
            return 0

        lax.fori_loop(0, Z, sib_wait, 0)

        def tile(i, cacc):
            rows = pl.ds(pl.multiple_of(i * BM, BM), BM)
            gt = jnp.dot(a_t[rows, :], call[:, cols_of(j)], preferred_element_type=F32)
            g_ref[rows, cols_of(j)] = gt
            sq = gt * gt
            row_acc[rows, :] += sum(sq[:, q * LANES:(q + 1) * LANES] for q in range(G))
            return cacc + jnp.sum(sq.reshape(BM // 8, 8, W), axis=0)

        cacc = lax.fori_loop(0, R // BM, tile, jnp.zeros((8, W), F32))
        csum = jnp.sum(cacc, axis=0, keepdims=True)
        for q in range(G):
            col_slots[me, pl.ds(j * G + q, 1), :] = csum[:, q * LANES:(q + 1) * LANES]
        return 0

    lax.fori_loop(0, NC, chunk, 0)

    for i in range(R // LANES):
        block = row_acc[i * LANES:(i + 1) * LANES, :].T
        row_slots[m, i:i + 1, :] = jnp.sum(block, axis=0, keepdims=True)

    def share(slots, send, recv, axis, own, count):
        def at(q):
            return remote(slots.at[own], slots.at[own], send.at[q], recv.at[own], **{axis: (own + q) % count})

        def go(q, _):
            at(q).start()
            return 0

        lax.fori_loop(1, count, go, 0)

    def shared(slots, send, recv, axis, own, count):
        def done(q, _):
            src = (own + q) % count
            remote(slots.at[src], slots.at[src], send.at[q], recv.at[src], **{axis: src}).wait_recv()
            return 0

        lax.fori_loop(1, count, done, 0)

    def sent(slots, send, recv, axis, own, count):
        def done(q, _):
            remote(slots.at[own], slots.at[own], send.at[q], recv.at[own], **{axis: (own + q) % count}).wait_send()
            return 0

        lax.fori_loop(1, count, done, 0)

    rows_x = (row_slots, row_send, row_recv, "mp", m, MP)
    cols_x = (col_slots, col_send, col_recv, "dp", me, DP)
    s_x = (s_slots, s_send, s_recv, "mp", m, MP)
    t_x = (t_slots, t_send, t_recv, "dp", me, DP)

    def total(slots, count):
        return lax.fori_loop(1, count, lambda i, a: a + slots[i], slots[0])

    share(*cols_x)
    share(*rows_x)
    shared(*rows_x)
    new_rows = decay_rate * rm_ref[...] + (1.0 - decay_rate) * ((total(row_slots, MP) + F * tiny_eps) / F)
    nr_ref[...] = new_rows
    inv_rows = 1.0 / new_rows
    for i in range(R // LANES):
        inv_r[i * LANES:(i + 1) * LANES, :] = jnp.broadcast_to(inv_rows[i:i + 1, :], (LANES, LANES)).T
    shared(*cols_x)
    new_cols = decay_rate * cm_ref[...] + (1.0 - decay_rate) * ((total(col_slots, DP) + D * tiny_eps) / D)
    nc_ref[...] = new_cols
    inv_c[...] = 1.0 / new_cols
    cs_ref[...] = lax.rsqrt(new_cols)

    def s_tile(i, acc):
        rows = pl.ds(pl.multiple_of(i * LANES, LANES), LANES)

        def s_cols(j, part):
            for q in range(G):
                v = g_ref[rows, pl.ds(pl.multiple_of(j * W + q * LANES, LANES), LANES)]
                part = part + (v * v) * inv_c[pl.ds(j * G + q, 1), :]
            return part

        part = lax.fori_loop(0, NC, s_cols, jnp.zeros((LANES, LANES), F32))
        return acc + jnp.sum((part * inv_r[rows, :]).reshape(LANES // 8, 8, LANES), axis=0)

    s_slots[m, 0] = lax.fori_loop(0, R // LANES, s_tile, jnp.zeros((8, LANES), F32))
    share(*s_x)
    rs_ref[...] = lax.sqrt(inv_r[...])
    t_slots[me, 2] = jnp.broadcast_to(jnp.sum(new_rows, axis=0, keepdims=True), (8, LANES))
    shared(*s_x)
    t_slots[me, 0:2] = total(s_slots, MP)
    share(*t_x)
    shared(*t_x)
    sums = total(t_slots, DP)

    def whole(v):
        return jnp.sum(jnp.sum(v, axis=0, keepdims=True), axis=1, keepdims=True)

    row_mean = whole(sums[2, 0:1, :]) / D
    update_rms = jnp.sqrt(row_mean * whole(sums[0]) / (D * F))
    weight_rms = jnp.sqrt(whole(sums[1]) / (D * F))
    factor = jnp.sqrt(row_mean) / jnp.maximum(1.0, update_rms)
    sc_ref[0:8, :] = jnp.broadcast_to(factor, (8, LANES))
    sc_ref[8:16, :] = jnp.broadcast_to(step_size * weight_rms, (8, LANES))

    sent(*rows_x)
    sent(*cols_x)
    sent(*s_x)
    sent(*t_x)

    def push_done(d, _):
        @pl.when(jnp.logical_and(d != me, taker(me, d) == m))
        def _():
            push(d).wait_send()

        @pl.when(jnp.logical_and(d != me, taker(d, me) == m))
        def _():
            def hand(q, _):
                spread(d, q).wait_send()
                return 0

            lax.fori_loop(1, MP, hand, 0)
        return 0

    lax.fori_loop(0, DP, push_done, 0)

    def cot_done(i, _):
        zs, j = i // NC, i % NC

        @pl.when(jnp.logical_and(zs <= z, z < Z - 1))
        def _():
            up(zs, j).wait_send()

        @pl.when(jnp.logical_and(zs >= z, z > 0))
        def _():
            down(zs, j).wait_send()

        across(zs, j).wait_send()
        return 0

    lax.fori_loop(0, Z * NC, cot_done, 0)


def apply_kernel(BR, g_ref, w_ref, rs_ref, cs_ref, sc_ref, nw_ref, up_ref):
    R, C = g_ref.shape

    def body(g, w, rs, nw, u):
        f1 = sc_ref[0:1, :]
        f2 = sc_ref[8:9, :]
        rscale = rs[...] * f1
        for q in range(C // LANES):
            sl = slice(q * LANES, (q + 1) * LANES)
            clipped = g[:, sl] * (rscale * cs_ref[q:q + 1, :])
            nw[:, sl] = w[:, sl] - f2 * clipped
            u[:, sl] = clipped.astype(u.dtype)

    wide = pl.BlockSpec((BR, C), lambda i: (i, 0))
    pltpu.emit_pipeline(
        body,
        grid=(R // BR,),
        in_specs=[wide, wide, pl.BlockSpec((BR, LANES), lambda i: (i, 0))],
        out_specs=[wide, wide],
    )(g_ref, w_ref, rs_ref, nw_ref, up_ref)


def on_device(MP, DP, inputs, cotangent, weight, row_moment, col_moment):
    T = inputs.shape[0]
    R, C = weight.shape
    Z = DP // 2
    W = min(512, C)
    NC = C // W
    BM = min(512, R)
    WB = min(128, R)
    RT, CT = R // LANES, C // LANES
    vmem = pl.BlockSpec(memory_space=pltpu.VMEM)
    hbm = pl.BlockSpec(memory_space=pl.ANY)
    dma = pltpu.SemaphoreType.DMA
    g, nr, nc, rs, cs, sc = pl.pallas_call(
        functools.partial(gather_kernel, MP, DP, W, BM),
        out_shape=[
            pltpu.VMEM((R, C), F32),
            jax.ShapeDtypeStruct((RT, LANES), F32),
            jax.ShapeDtypeStruct((CT, LANES), F32),
            pltpu.VMEM((R, LANES), F32),
            pltpu.VMEM((CT, LANES), F32),
            pltpu.VMEM((16, LANES), F32),
        ],
        in_specs=[hbm, hbm, hbm, vmem, vmem],
        out_specs=[vmem] * 6,
        scratch_shapes=[
            pltpu.VMEM((T * DP, R), jnp.bfloat16),
            pltpu.VMEM((R, T * DP), jnp.bfloat16),
            pltpu.VMEM((T * DP, C), jnp.bfloat16),
            pltpu.VMEM((2, WB, C), F32),
            pltpu.VMEM((R, LANES), F32),
            pltpu.VMEM((R, LANES), F32),
            pltpu.VMEM((CT, LANES), F32),
            pltpu.VMEM((MP, RT, LANES), F32),
            pltpu.VMEM((DP, CT, LANES), F32),
            pltpu.VMEM((MP, 2, 8, LANES), F32),
            pltpu.VMEM((DP, 3, 8, LANES), F32),
            dma((2,)), dma((2,)), dma((DP,)), dma((DP,)), dma((DP, MP)),
            dma((Z, NC)), dma((Z, NC)), dma((Z, NC)), dma((Z, NC)), dma((Z, NC)),
            dma((MP,)), dma((MP,)), dma((DP,)), dma((DP,)),
            dma((MP,)), dma((MP,)), dma((DP,)), dma((DP,)),
        ],
        compiler_params=pltpu.CompilerParams(
            collective_id=0, has_side_effects=True, vmem_limit_bytes=44 * 2**20
        ),
        cost_estimate=pl.CostEstimate(flops=2 * R * C * T * DP, bytes_accessed=R * C * 4, transcendentals=0),
        name="gather_contract",
    )(inputs, cotangent, weight, row_moment.reshape(RT, LANES), col_moment.reshape(CT, LANES))
    BR = min(64, R)
    new_weight, update = pl.pallas_call(
        functools.partial(apply_kernel, BR),
        out_shape=[jax.ShapeDtypeStruct((R, C), F32), jax.ShapeDtypeStruct((R, C), jnp.bfloat16)],
        in_specs=[vmem, hbm, vmem, vmem, vmem],
        out_specs=[hbm, hbm],
        compiler_params=pltpu.CompilerParams(vmem_limit_bytes=32 * 2**20),
        cost_estimate=pl.CostEstimate(flops=4 * R * C, bytes_accessed=R * C * 10, transcendentals=0),
        name="apply_update",
    )(g, weight, rs, cs, sc)
    return new_weight, update, nr.reshape(R), nc.reshape(C)


def solution(mesh):
    return jax.shard_map(
        functools.partial(on_device, mesh.shape["mp"], mesh.shape["dp"]),
        mesh=mesh,
        in_specs=(P("dp", None), P("dp", "mp"), P("dp", "mp"), P("dp"), P("mp")),
        out_specs=(P("dp", "mp"), P("dp", "mp"), P("dp"), P("mp")),
        check_vma=False,
    )
```

time: 297 us -> 161 us (0.54)
  Pallas kernels: 0 us -> 147 us
  waiting for transfers between devices: 135 us -> 0 us
  blocking collectives: 74.8 us -> 0 us
  other arithmetic: 41.3 us -> 0 us
  matrix products: 18.7 us -> 0 us
  between operations: 16.1 us -> 0.65 us
  local copies, waits for them, and re-layouts: 3.59 us -> 13.1 us
  starting transfers between devices: 6.36 us -> 0 us
    pallas_call x0 -> x2, Pallas kernels: none -> 147 us  [the longest x1 127 us: on_device(): pl.pallas_call(functools.partial(gather_kernel, MP, DP, W, BM), out_shape...]
    all_to_all x1 -> x0, waiting for transfers between devices: 117 us -> none  [on_device(): lax.all_to_all(inputs, 'dp', split_axis=1, concat_axis=0, tiled=True)]
    psum x3 -> x0, blocking collectives: 74.8 us -> none  [the longest x1 37.1 us: on_device(): scaled_sq = lax.psum(jnp.sum(scaled * scaled), ('mp', 'dp'))]
    reduce_sum x3 -> x0, other arithmetic: 22 us -> none  [the longest x1 12.4 us: on_device(): weight_sq = jnp.sum(weight * weight)]
    convert_element_type x1 -> x0, other arithmetic: 19.3 us -> none  [on_device(): return (new_weight, clipped.astype(jnp.bfloat16), new_rows, new_cols)]
    dot_general x1 -> x0, matrix products: 18.7 us -> none  [contract(): lax.dot_general(left, right, (((0,), (0,)), ((), ())), preferred_element_...]
    all_gather x1 -> x0, waiting for transfers between devices: 17.3 us -> none  [on_device(): lax.all_gather(cotangent, 'dp', axis=0, tiled=True)]
    unnamed x8 -> x10, local copies, waits for them, and re-layouts: 0.02 us -> 13.1 us
  transfers between devices with their start and end apart: 2 -> 0, of which waited for: 2 -> 0; matrix products, arithmetic and copies ran while one was open for 5% -> 0% of each run, Pallas kernels for 0% -> 0%
where the time goes in v1:
time: 161 us
  Pallas kernels  147 us (91%)
  local copies, waits for them, and re-layouts  13.1 us (8%)
    pallas_call x1, Pallas kernels, on_device(): pl.pallas_call(functools.partial(gather_kernel, MP, DP, W, BM), out_shape...  127 us
    pallas_call x1, Pallas kernels, on_device(): pl.pallas_call(functools.partial(apply_kernel, BR), out_shape=[jax.ShapeD...  19.4 us
    unnamed x10, local copies, waits for them, and re-layouts  13.1 us

profile of v1, /device:TPU:0, one launch (start us, length us, event | category | flops | bytes accessed | tf_op | source)
XLA Modules:
  0.0 160.6 jit_solution(10544884527970387258)
XLA Ops:
  0.6 127.4 %gather_contract.1 = (f32[1024,4096]{1,0:T(8,128)S(1)}, f32[8,128]{1,0:T(8,128)}, f32[32,128]{1,0:T(8,128)}, f32[1024,128]{1,0:T(8,128)S(1)}, f32[32,128]{1,0:T(8,128)S(1)}, /*index=5*/f32[16,128]{1,0:T(8,128)S(1)}) custom-call(bf16[160,8192]{1,0:T(8,128)(2,1)} %x_ref.1, bf16[160,4096]{1,0:T(8,128)(2,1)} %cot_ref.1, f32[1024,4096]{1,0:T(8,128)} %w_ref.3, ...), custom_call_target="tpu_custom_call" | custom-call | flops 10737418240 | bytes 16777216 | tf_op jit(solution)/shard_map/gather_contract/pallas_call | solution.py:395
  128.0 0.0 copy-start
  128.0 6.2 %copy-done = f32[1024,4096]{1,0:T(8,128)} copy-done((f32[1024,4096]{1,0:T(8,128)}, f32[1024,4096]{1,0:T(8,128)S(1)}, u32[]{:S(2)}) %copy-start) | copy-done | bytes 16777240
  134.2 0.0 copy-start.1
  134.2 5.8 %copy-done.1 = f32[1024,4096]{1,0:T(8,128)S(1)} copy-done((f32[1024,4096]{1,0:T(8,128)S(1)}, f32[1024,4096]{1,0:T(8,128)}, u32[]{:S(2)}) %copy-start.1) | copy-done | bytes 16777240
  140.0 0.0 copy-start.3
  140.0 0.0 copy-start.2
  140.0 19.4 %apply_update.1 = (f32[1024,4096]{1,0:T(8,128)}, bf16[1024,4096]{1,0:T(8,128)(2,1)}) custom-call(f32[1024,4096]{1,0:T(8,128)S(1)} %copy-done.1, f32[1024,4096]{1,0:T(8,128)} %w_ref.3, f32[1024,128]{1,0:T(8,128)S(1)} %get-tuple-element.13.rs_ref, f32[32,128]{1,0:T(8,128)S(1)} %get-tuple-element.14.cs_ref, f32[16,128]{1,0:T(8,128)S(1)} %get-tuple-element.15.sc_ref), custom_call_target="tpu_custom_call" | custom-call | flops 16777216 | bytes 41943040 | tf_op jit(solution)/shard_map/apply_update/pallas_call | solution.py:431
  159.3 0.0 copy-done.3
  159.3 0.6 copy.11
  159.9 0.0 copy-done.2
  159.9 0.6 copy.12
Async XLA Ops:
  128.0 6.2 %copy-start = (f32[1024,4096]{1,0:T(8,128)}, f32[1024,4096]{1,0:T(8,128)S(1)}, u32[]{:S(2)}) copy-start(f32[1024,4096]{1,0:T(8,128)S(1)} %get-tuple-element.12.g_ref) | copy-start | bytes 50331652
  134.2 5.8 %copy-start.1 = (f32[1024,4096]{1,0:T(8,128)S(1)}, f32[1024,4096]{1,0:T(8,128)}, u32[]{:S(2)}) copy-start(f32[1024,4096]{1,0:T(8,128)} %copy-done) | copy-start | bytes 50331652
  140.0 19.4 %copy-start.3 = (f32[8,128]{1,0:T(8,128)S(1)}, f32[8,128]{1,0:T(8,128)}, u32[]{:S(2)}) copy-start(f32[8,128]{1,0:T(8,128)} %get-tuple-element.18) | copy-start | bytes 12292
  140.0 20.0 %copy-start.2 = (f32[32,128]{1,0:T(8,128)S(1)}, f32[32,128]{1,0:T(8,128)}, u32[]{:S(2)}) copy-start(f32[32,128]{1,0:T(8,128)} %get-tuple-element.19) | copy-start | bytes 49156

commit v2 on v1

v2 whole, which is shorter than its diff:
```python
import functools

import jax
import jax.numpy as jnp
from jax import lax
from jax.experimental import pallas as pl
from jax.experimental.pallas import tpu as pltpu
from jax.sharding import PartitionSpec as P

decay_rate = 1.0 - 10.0 ** (-0.8)
step_size = 0.05
tiny_eps = 1e-30

LANES = 128
MESH = pl.DeviceIdType.MESH
F32 = jnp.float32


def gather_kernel(
    MP, DP, W, BM, LAG,
    x_ref, cot_ref, w_ref, rm_ref, cm_ref,
    buf,
    a_raw, a_t, call, row_acc, s_acc, inv_r, n_cols, row_slots, col_slots, s_slots, t_slots,
    own_sem, in_send, in_recv, fwd_send, up_send, dn_send, sib_send,
    lane_recv, sib_recv, row_send, row_recv, col_send, col_recv,
    s_send, s_recv, t_send, t_recv,
):
    m = lax.axis_index("mp")
    me = lax.axis_index("dp")
    z, c = me // 2, me % 2
    Z = DP // 2
    sib = me + 1 - 2 * c
    T = x_ref.shape[0]
    R, C = w_ref.shape
    RT, CT = R // LANES, C // LANES
    NC = C // W
    G = W // LANES
    D, F = R * DP, C * MP
    at_rows, at_cols, at_scale = extras(R, C)

    barrier = pltpu.get_barrier_semaphore()

    def greet_dp(q, _):
        pl.semaphore_signal(barrier, inc=1, device_id={"dp": (me + q) % DP}, device_id_type=MESH)
        return 0

    def greet_mp(q, _):
        pl.semaphore_signal(barrier, inc=1, device_id={"mp": (m + q) % MP}, device_id_type=MESH)
        return 0

    lax.fori_loop(1, DP, greet_dp, 0)
    lax.fori_loop(1, MP, greet_mp, 0)

    def rows_of(s):
        return pl.ds(pl.multiple_of(s * T, T), T)

    def cols_of(j):
        return pl.ds(pl.multiple_of(j * W, W), W)

    def feat_cols(d):
        return pl.ds(pl.multiple_of(d * R, R), R)

    own_x = pltpu.make_async_copy(x_ref.at[:, feat_cols(me)], a_raw.at[rows_of(me), :], own_sem.at[0])
    own_c = pltpu.make_async_copy(cot_ref, call.at[rows_of(me), :], own_sem.at[1])
    own_w = pltpu.make_async_copy(w_ref, buf.at[pl.ds(R, R), :], own_sem.at[2])
    own_x.start()
    own_c.start()
    pl.semaphore_wait(barrier, DP + MP - 2)

    def remote(src, dst, send, recv, **to):
        return pltpu.make_async_remote_copy(
            src_ref=src, dst_ref=dst, send_sem=send, recv_sem=recv,
            device_id=to, device_id_type=MESH,
        )

    def taker(s, d):
        return (s + (MP // 2) * (d % 2)) % MP

    def push(d):
        return remote(x_ref.at[:, feat_cols(d)], a_raw.at[rows_of(me), :],
                      in_send.at[d], in_recv.at[me], dp=d)

    def spread(s, q):
        return remote(a_raw.at[rows_of(s), :], a_raw.at[rows_of(s), :],
                      fwd_send.at[s, q], in_recv.at[s], mp=(m + q) % MP)

    def cot_block(zs, lane, j):
        return call.at[rows_of(zs * 2 + lane), cols_of(j)]

    def up(zs, j, src=None):
        dst = cot_block(zs, c, j)
        return remote(dst if src is None else src, dst, up_send.at[zs, j], lane_recv.at[zs, j], dp=(me + 2) % DP)

    def down(zs, j, src=None):
        dst = cot_block(zs, c, j)
        return remote(dst if src is None else src, dst, dn_send.at[zs, j], lane_recv.at[zs, j], dp=(me + DP - 2) % DP)

    def across(zs, j, src=None):
        dst = cot_block(zs, c, j)
        return remote(dst if src is None else src, dst, sib_send.at[zs, j], sib_recv.at[zs, j], dp=sib)

    def across_in(zs, j):
        dst = cot_block(zs, 1 - c, j)
        return remote(dst, dst, sib_send.at[zs, j], sib_recv.at[zs, j], dp=sib)

    def push_step(d, _):
        @pl.when(jnp.logical_and(d != me, taker(me, d) == m))
        def _():
            push(d).start()
        return 0

    lax.fori_loop(0, DP, push_step, 0)

    DEPTH = 3

    def paced(n):
        k, j = n // NC, n % NC

        @pl.when(n >= 0)
        def _():
            @pl.when(jnp.logical_and(z - k >= 0, z < Z - 1))
            def _():
                up(z - k, j).wait_send()

            @pl.when(jnp.logical_and(z + k < Z, z > 0))
            def _():
                down(z + k, j).wait_send()

    def first_send(j, _):
        src = cot_ref.at[:, cols_of(j)]
        paced(j - DEPTH)

        @pl.when(z < Z - 1)
        def _():
            up(z, j, src).start()

        @pl.when(z > 0)
        def _():
            down(z, j, src).start()

        across(z, j, src).start()
        return 0

    def take_step(s, _):
        @pl.when(jnp.logical_and(s != me, taker(s, me) == m))
        def _():
            spread(s, 1).wait_recv()

            def hand(q, _):
                spread(s, q).start()
                return 0

            lax.fori_loop(1, MP, hand, 0)
        return 0

    early = min(5, NC)
    lax.fori_loop(0, early, first_send, 0)
    own_w.start()
    lax.fori_loop(0, DP, take_step, 0)
    lax.fori_loop(early, NC, first_send, 0)

    def relay(k, j):
        lo, hi = z - k, z + k
        paced(k * NC + j - DEPTH)

        @pl.when(lo >= 0)
        def _():
            up(lo, j).wait_recv()

            @pl.when(z < Z - 1)
            def _():
                up(lo, j).start()

            across(lo, j).start()

        @pl.when(hi < Z)
        def _():
            down(hi, j).wait_recv()

            @pl.when(z > 0)
            def _():
                down(hi, j).start()

            across(hi, j).start()

    def weight_step(j, acc):
        relay(1, j)
        v = buf[R:2 * R, cols_of(j)]
        return acc + jnp.sum((v * v).reshape(R // 8, 8, W), axis=0)

    own_w.wait()
    wacc = lax.fori_loop(0, NC, weight_step, jnp.zeros((8, W), F32))
    s_slots[m, 1] = sum(wacc[:, q * LANES:(q + 1) * LANES] for q in range(G))

    def relay_step(i, _):
        relay(2 + i // NC, i % NC)
        return 0

    lax.fori_loop(0, (Z // 2 - 2) * NC, relay_step, 0)

    def rest_step(s, _):
        @pl.when(jnp.logical_and(s != me, taker(s, me) != m))
        def _():
            spread(s, 1).wait_recv()
        return 0

    lax.fori_loop(0, DP, rest_step, 0)
    own_x.wait()
    own_c.wait()

    def turn(i, _):
        cols = pl.ds(pl.multiple_of(i * LANES, LANES), LANES)
        a_t[cols, :] = a_raw[:, cols].T
        return 0

    lax.fori_loop(0, R // LANES, turn, 0)
    row_acc[...] = jnp.zeros_like(row_acc)
    s_acc[...] = jnp.zeros_like(s_acc)

    def col_rows(j):
        return pl.ds(pl.multiple_of(j * G, G), G)

    def col_copy(q, j, own):
        return remote(col_slots.at[own, j], col_slots.at[own, j],
                      col_send.at[q, j], col_recv.at[own, j], dp=(me + q) % DP)

    def s_part(j):
        def got(q, _):
            col_copy(q, j, (me + q) % DP).wait_recv()
            return 0

        lax.fori_loop(1, DP, got, 0)
        tot = lax.fori_loop(1, DP, lambda i, a: a + col_slots[i, j], col_slots[0, j])
        mean = (tot + D * tiny_eps) / D
        inv = []
        for q in range(G):
            row = pl.ds(j * G + q, 1)
            new_cols = decay_rate * cm_ref[row, :] + (1.0 - decay_rate) * mean[q:q + 1, :]
            n_cols[row, :] = new_cols
            inv.append(1.0 / new_cols)

        def s_tile(i, _):
            rows = pl.ds(pl.multiple_of(i * LANES, LANES), LANES)
            part = s_acc[rows, :]
            for q in range(G):
                v = buf[rows, pl.ds(pl.multiple_of(j * W + q * LANES, LANES), LANES)]
                part = part + (v * v) * inv[q]
            s_acc[rows, :] = part
            return 0

        lax.fori_loop(0, RT, s_tile, 0)

    def chunk(j):
        def sib_wait(zs, _):
            @pl.when(zs >= 0)
            def _():
                across_in(zs, j).wait_recv()
            return 0

        lax.fori_loop(0, Z, sib_wait, 0)

        def tile(i, cacc):
            rows = pl.ds(pl.multiple_of(i * BM, BM), BM)
            gt = jnp.dot(a_t[rows, :], call[:, cols_of(j)], preferred_element_type=F32)
            buf[rows, cols_of(j)] = gt
            sq = gt * gt
            row_acc[rows, :] += sum(sq[:, q * LANES:(q + 1) * LANES] for q in range(G))
            return cacc + jnp.sum(sq.reshape(BM // 8, 8, W), axis=0)

        cacc = lax.fori_loop(0, R // BM, tile, jnp.zeros((8, W), F32))
        csum = jnp.sum(cacc, axis=0, keepdims=True)
        for q in range(G):
            col_slots[me, j, q:q + 1, :] = csum[:, q * LANES:(q + 1) * LANES]

        def go(q, _):
            col_copy(q, j, me).start()
            return 0

        lax.fori_loop(1, DP, go, 0)

        @pl.when(j >= LAG)
        def _():
            s_part(j - LAG)

    last = jnp.maximum(z, Z - 1 - z)

    def work_step(i, _):
        k, j = Z // 2 + i // NC, i % NC
        relay(k, j)

        @pl.when(k == last)
        def _():
            chunk(j)
        return 0

    lax.fori_loop(0, (Z - Z // 2) * NC, work_step, 0)

    for i in range(RT):
        block = row_acc[i * LANES:(i + 1) * LANES, :].T
        row_slots[m, i:i + 1, :] = jnp.sum(block, axis=0, keepdims=True)

    def share(slots, send, recv, axis, own, count):
        def go(q, _):
            remote(slots.at[own], slots.at[own], send.at[q], recv.at[own], **{axis: (own + q) % count}).start()
            return 0

        lax.fori_loop(1, count, go, 0)

    def shared(slots, send, recv, axis, own, count):
        def done(q, _):
            src = (own + q) % count
            remote(slots.at[src], slots.at[src], send.at[q], recv.at[src], **{axis: src}).wait_recv()
            return 0

        lax.fori_loop(1, count, done, 0)

    def sent(slots, send, recv, axis, own, count):
        def done(q, _):
            remote(slots.at[own], slots.at[own], send.at[q], recv.at[own], **{axis: (own + q) % count}).wait_send()
            return 0

        lax.fori_loop(1, count, done, 0)

    rows_x = (row_slots, row_send, row_recv, "mp", m, MP)
    s_x = (s_slots, s_send, s_recv, "mp", m, MP)
    t_x = (t_slots, t_send, t_recv, "dp", me, DP)

    def total(slots, count):
        return lax.fori_loop(1, count, lambda i, a: a + slots[i], slots[0])

    share(*rows_x)

    def s_rest(j, _):
        s_part(j)
        return 0

    shared(*rows_x)
    new_rows = decay_rate * rm_ref[...] + (1.0 - decay_rate) * ((total(row_slots, MP) + F * tiny_eps) / F)
    buf[at_rows:at_rows + RT, 0:LANES] = new_rows
    inv_rows = 1.0 / new_rows
    for i in range(RT):
        inv_r[i * LANES:(i + 1) * LANES, :] = jnp.broadcast_to(inv_rows[i:i + 1, :], (LANES, LANES)).T
    lax.fori_loop(NC - LAG, NC, s_rest, 0)
    buf[at_cols:at_cols + CT, 0:LANES] = n_cols[...]

    s_slots[m, 0] = jnp.sum((s_acc[...] * inv_r[...]).reshape(R // 8, 8, LANES), axis=0)
    share(*s_x)
    t_slots[me, 2] = jnp.broadcast_to(jnp.sum(new_rows, axis=0, keepdims=True), (8, LANES))
    shared(*s_x)
    t_slots[me, 0:2] = total(s_slots, MP)
    share(*t_x)

    sent(*rows_x)
    sent(*s_x)

    def push_done(d, _):
        @pl.when(jnp.logical_and(d != me, taker(me, d) == m))
        def _():
            push(d).wait_send()

        @pl.when(jnp.logical_and(d != me, taker(d, me) == m))
        def _():
            def hand(q, _):
                spread(d, q).wait_send()
                return 0

            lax.fori_loop(1, MP, hand, 0)
        return 0

    lax.fori_loop(0, DP, push_done, 0)

    def cot_done(i, _):
        across(i // NC, i % NC).wait_send()
        return 0

    lax.fori_loop(0, Z * NC, cot_done, 0)

    def tail_done(i, _):
        paced(Z * NC - DEPTH + i)
        return 0

    lax.fori_loop(0, DEPTH, tail_done, 0)

    def col_done(i, _):
        col_copy(1 + i // NC, i % NC, me).wait_send()
        return 0

    lax.fori_loop(0, (DP - 1) * NC, col_done, 0)

    shared(*t_x)
    sums = total(t_slots, DP)

    def whole(v):
        return jnp.sum(jnp.sum(v, axis=0, keepdims=True), axis=1, keepdims=True)

    row_mean = whole(sums[2, 0:1, :]) / D
    update_rms = jnp.sqrt(row_mean * whole(sums[0]) / (D * F))
    weight_rms = jnp.sqrt(whole(sums[1]) / (D * F))
    factor = jnp.sqrt(row_mean) / jnp.maximum(1.0, update_rms)
    buf[at_scale:at_scale + 8, 0:LANES] = jnp.broadcast_to(factor, (8, LANES))
    buf[at_scale + 8:at_scale + 16, 0:LANES] = jnp.broadcast_to(step_size * weight_rms, (8, LANES))
    sent(*t_x)


def extras(R, C):
    RT, CT = R // LANES, C // LANES
    at_rows = 2 * R
    at_cols = at_rows + -(-RT // 8) * 8
    return at_rows, at_cols, at_cols + -(-CT // 8) * 8


def apply_kernel(R, C, BR, SLOTS, buf, nw_ref, up_ref, nr_ref, nc_ref, rs, cs, nw_buf, up_buf, nw_sem, up_sem):
    RT, CT = R // LANES, C // LANES
    at_rows, at_cols, at_scale = extras(R, C)
    f1 = buf[at_scale:at_scale + 1, 0:LANES]
    f2 = buf[at_scale + 8:at_scale + 9, 0:LANES]
    new_rows = buf[at_rows:at_rows + RT, 0:LANES]
    new_cols = buf[at_cols:at_cols + CT, 0:LANES]
    nr_ref[...] = new_rows
    nc_ref[...] = new_cols
    cs[...] = lax.rsqrt(new_cols)
    inv = lax.rsqrt(new_rows) * f1
    for i in range(RT):
        rs[i * LANES:(i + 1) * LANES, :] = jnp.broadcast_to(inv[i:i + 1, :], (LANES, LANES)).T
    N = R // BR

    def out_copies(i, slot):
        rows = pl.ds(pl.multiple_of(i * BR, BR), BR)
        return (
            pltpu.make_async_copy(nw_buf.at[slot], nw_ref.at[rows, :], nw_sem.at[slot]),
            pltpu.make_async_copy(up_buf.at[slot], up_ref.at[rows, :], up_sem.at[slot]),
        )

    def step(i, _):
        slot = lax.rem(i, SLOTS)

        @pl.when(i >= SLOTS)
        def _():
            for copy in out_copies(i - SLOTS, slot):
                copy.wait()

        g_rows = pl.ds(pl.multiple_of(i * BR, BR), BR)
        w_rows = pl.ds(pl.multiple_of(R + i * BR, BR), BR)
        scale = rs[g_rows, :]
        for q in range(CT):
            sl = slice(q * LANES, (q + 1) * LANES)
            clipped = buf[g_rows, sl] * (scale * cs[q:q + 1, :])
            nw_buf[slot, :, sl] = buf[w_rows, sl] - f2 * clipped
            up_buf[slot, :, sl] = clipped.astype(up_buf.dtype)
        for copy in out_copies(i, slot):
            copy.start()
        return 0

    lax.fori_loop(0, N, step, 0)

    def drain(i, _):
        for copy in out_copies(i, lax.rem(i, SLOTS)):
            copy.wait()
        return 0

    lax.fori_loop(N - SLOTS, N, drain, 0)


def on_device(MP, DP, inputs, cotangent, weight, row_moment, col_moment):
    T = inputs.shape[0]
    R, C = weight.shape
    Z = DP // 2
    W = min(512, C)
    NC = C // W
    G = W // LANES
    BM = min(512, R)
    RT, CT = R // LANES, C // LANES
    height = extras(R, C)[2] + 16
    vmem = pl.BlockSpec(memory_space=pltpu.VMEM)
    hbm = pl.BlockSpec(memory_space=pl.ANY)
    dma = pltpu.SemaphoreType.DMA
    buf = pl.pallas_call(
        functools.partial(gather_kernel, MP, DP, W, BM, min(4, NC)),
        out_shape=pltpu.VMEM((height, C), F32),
        in_specs=[hbm, hbm, hbm, vmem, vmem],
        out_specs=vmem,
        scratch_shapes=[
            pltpu.VMEM((T * DP, R), jnp.bfloat16),
            pltpu.VMEM((R, T * DP), jnp.bfloat16),
            pltpu.VMEM((T * DP, C), jnp.bfloat16),
            pltpu.VMEM((R, LANES), F32),
            pltpu.VMEM((R, LANES), F32),
            pltpu.VMEM((R, LANES), F32),
            pltpu.VMEM((CT, LANES), F32),
            pltpu.VMEM((MP, RT, LANES), F32),
            pltpu.VMEM((DP, NC, G, LANES), F32),
            pltpu.VMEM((MP, 2, 8, LANES), F32),
            pltpu.VMEM((DP, 3, 8, LANES), F32),
            dma((3,)), dma((DP,)), dma((DP,)), dma((DP, MP)),
            dma((Z, NC)), dma((Z, NC)), dma((Z, NC)), dma((Z, NC)), dma((Z, NC)),
            dma((MP,)), dma((MP,)), dma((DP, NC)), dma((DP, NC)),
            dma((MP,)), dma((MP,)), dma((DP,)), dma((DP,)),
        ],
        compiler_params=pltpu.CompilerParams(
            collective_id=0, has_side_effects=True, vmem_limit_bytes=28 * 2**20
        ),
        cost_estimate=pl.CostEstimate(flops=2 * R * C * T * DP, bytes_accessed=R * C * 4, transcendentals=0),
        name="gather_contract",
    )(inputs, cotangent, weight, row_moment.reshape(RT, LANES), col_moment.reshape(CT, LANES))
    BR = min(64, R)
    SLOTS = min(3, R // BR)
    new_weight, update, nr, nc = pl.pallas_call(
        functools.partial(apply_kernel, R, C, BR, SLOTS),
        out_shape=[
            jax.ShapeDtypeStruct((R, C), F32),
            jax.ShapeDtypeStruct((R, C), jnp.bfloat16),
            jax.ShapeDtypeStruct((RT, LANES), F32),
            jax.ShapeDtypeStruct((CT, LANES), F32),
        ],
        in_specs=[vmem],
        out_specs=[hbm, hbm, vmem, vmem],
        scratch_shapes=[
            pltpu.VMEM((R, LANES), F32),
            pltpu.VMEM((CT, LANES), F32),
            pltpu.VMEM((SLOTS, BR, C), F32),
            pltpu.VMEM((SLOTS, BR, C), jnp.bfloat16),
            dma((SLOTS,)), dma((SLOTS,)),
        ],
        compiler_params=pltpu.CompilerParams(vmem_limit_bytes=16 * 2**20),
        cost_estimate=pl.CostEstimate(flops=4 * R * C, bytes_accessed=R * C * 6, transcendentals=0),
        name="apply_update",
    )(buf)
    return new_weight, update, nr.reshape(R), nc.reshape(C)


def solution(mesh):
    return jax.shard_map(
        functools.partial(on_device, mesh.shape["mp"], mesh.shape["dp"]),
        mesh=mesh,
        in_specs=(P("dp", None), P("dp", "mp"), P("dp", "mp"), P("dp"), P("mp")),
        out_specs=(P("dp", "mp"), P("dp", "mp"), P("dp"), P("mp")),
        check_vma=False,
    )
```

time: 161 us -> 134 us (0.83)
  Pallas kernels: 147 us -> 133 us
  local copies, waits for them, and re-layouts: 13.1 us -> 0 us
    pallas_call x2, Pallas kernels: 147 us -> 133 us  [the longest x1 123 us: on_device(): pl.pallas_call(functools.partial(gather_kernel, MP, DP, W, BM, min(4, NC)...]
    unnamed x10 -> x0, local copies, waits for them, and re-layouts: 13.1 us -> none
where the time goes in v2:
time: 134 us; the launch traced here: 133 us
  Pallas kernels  133 us (99%)
    pallas_call x1, Pallas kernels, on_device(): pl.pallas_call(functools.partial(gather_kernel, MP, DP, W, BM, min(4, NC)...  123 us
    pallas_call x1, Pallas kernels, on_device(): pl.pallas_call(functools.partial(apply_kernel, R, C, BR, SLOTS), out_shap...  9.42 us

profile of v2, /device:TPU:0, one launch (start us, length us, event | category | flops | bytes accessed | tf_op | source)
XLA Modules:
  0.0 133.3 jit_solution(8854419204496460753)
XLA Ops:
  0.6 123.3 %gather_contract.1.buf = f32[2104,4096]{1,0:T(8,128)S(1)} custom-call(bf16[160,8192]{1,0:T(8,128)(2,1)} %x_ref.1, bf16[160,4096]{1,0:T(8,128)(2,1)} %cot_ref.1, f32[1024,4096]{1,0:T(8,128)} %w_ref.1, f32[8,128]{1,0:T(8,128)} %bitcast.5, f32[32,128]{1,0:T(8,128)} %bitcast.4), custom_call_target="tpu_custom_call" | custom-call | flops 10737418240 | bytes 16777216 | tf_op jit(solution)/shard_map/gather_contract/pallas_call | solution.py:477
  123.9 9.4 %apply_update.1 = (f32[1024,4096]{1,0:T(8,128)}, bf16[1024,4096]{1,0:T(8,128)(2,1)}, f32[8,128]{1,0:T(8,128)}, f32[32,128]{1,0:T(8,128)}) custom-call(f32[2104,4096]{1,0:T(8,128)S(1)} %gather_contract.1.buf), custom_call_target="tpu_custom_call" | custom-call | flops 16777216 | bytes 25165824 | tf_op jit(solution)/shard_map/apply_update/pallas_call | solution.py:507

commit v3 on v2

--- a/solution.py
+++ b/solution.py
@@ -20,8 +20,8 @@
     MP, DP, W, BM, LAG,
     x_ref, cot_ref, w_ref, rm_ref, cm_ref,
     buf,
-    a_raw, a_t, call, row_acc, s_acc, inv_r, n_cols, row_slots, col_slots, s_slots, t_slots,
-    own_sem, in_send, in_recv, fwd_send, up_send, dn_send, sib_send,
+    a_raw, a_near, a_far, call, row_acc, s_acc, inv_r, n_cols, row_slots, col_slots, s_slots, t_slots,
+    own_sem, own_csem, in_send, in_recv, fwd_send, up_send, dn_send, sib_send,
     lane_recv, sib_recv, row_send, row_recv, col_send, col_recv,
     s_send, s_recv, t_send, t_recv,
 ):
@@ -61,10 +61,12 @@
         return pl.ds(pl.multiple_of(d * R, R), R)
 
     own_x = pltpu.make_async_copy(x_ref.at[:, feat_cols(me)], a_raw.at[rows_of(me), :], own_sem.at[0])
-    own_c = pltpu.make_async_copy(cot_ref, call.at[rows_of(me), :], own_sem.at[1])
-    own_w = pltpu.make_async_copy(w_ref, buf.at[pl.ds(R, R), :], own_sem.at[2])
+    own_w = pltpu.make_async_copy(w_ref, buf.at[pl.ds(R, R), :], own_sem.at[1])
     own_x.start()
-    own_c.start()
+
+    def own_c(j):
+        return pltpu.make_async_copy(cot_ref.at[:, cols_of(j)], call.at[j, rows_of(me), :], own_csem.at[j])
+
     pl.semaphore_wait(barrier, DP + MP - 2)
 
     def remote(src, dst, send, recv, **to):
@@ -85,7 +87,7 @@
                       fwd_send.at[s, q], in_recv.at[s], mp=(m + q) % MP)
 
     def cot_block(zs, lane, j):
-        return call.at[rows_of(zs * 2 + lane), cols_of(j)]
+        return call.at[j, rows_of(zs * 2 + lane), :]
 
     def up(zs, j, src=None):
         dst = cot_block(zs, c, j)
@@ -111,7 +113,7 @@
 
     lax.fori_loop(0, DP, push_step, 0)
 
-    DEPTH = 3
+    DEPTH = 6
 
     def paced(n):
         k, j = n // NC, n % NC
@@ -139,6 +141,7 @@
             down(z, j, src).start()
 
         across(z, j, src).start()
+        own_c(j).start()
         return 0
 
     def take_step(s, _):
@@ -206,11 +209,21 @@
 
     lax.fori_loop(0, DP, rest_step, 0)
     own_x.wait()
-    own_c.wait()
+
+    def own_done(j, _):
+        own_c(j).wait()
+        return 0
+
+    lax.fori_loop(0, NC, own_done, 0)
+
+    far_z = jnp.where(z >= Z // 2, 0, Z - 1)
+    far_rows = pl.ds(pl.multiple_of(far_z * 2 * T, 2 * T), 2 * T)
+    near_rows = pl.ds(pl.multiple_of(jnp.where(z >= Z // 2, 2 * T, 0), 2 * T), (Z - 1) * 2 * T)
 
     def turn(i, _):
         cols = pl.ds(pl.multiple_of(i * LANES, LANES), LANES)
-        a_t[cols, :] = a_raw[:, cols].T
+        a_near[cols, :] = a_raw[near_rows, cols].T
+        a_far[cols, :] = a_raw[far_rows, cols].T
         return 0
 
     lax.fori_loop(0, R // LANES, turn, 0)
@@ -250,18 +263,28 @@
 
         lax.fori_loop(0, RT, s_tile, 0)
 
-    def chunk(j):
+    def near(j):
         def sib_wait(zs, _):
-            @pl.when(zs >= 0)
+            @pl.when(zs != far_z)
             def _():
                 across_in(zs, j).wait_recv()
             return 0
 
         lax.fori_loop(0, Z, sib_wait, 0)
 
+        def tile(i, _):
+            rows = pl.ds(pl.multiple_of(i * BM, BM), BM)
+            buf[rows, cols_of(j)] = jnp.dot(a_near[rows, :], call[j, near_rows, :], preferred_element_type=F32)
+            return 0
+
+        lax.fori_loop(0, R // BM, tile, 0)
+
+    def chunk(j):
+        across_in(far_z, j).wait_recv()
+
         def tile(i, cacc):
             rows = pl.ds(pl.multiple_of(i * BM, BM), BM)
-            gt = jnp.dot(a_t[rows, :], call[:, cols_of(j)], preferred_element_type=F32)
+            gt = buf[rows, cols_of(j)] + jnp.dot(a_far[rows, :], call[j, far_rows, :], preferred_element_type=F32)
             buf[rows, cols_of(j)] = gt
             sq = gt * gt
             row_acc[rows, :] += sum(sq[:, q * LANES:(q + 1) * LANES] for q in range(G))
@@ -284,16 +307,33 @@
 
     last = jnp.maximum(z, Z - 1 - z)
 
+    ahead = jnp.where(last == Z - 1, 0, min(2, NC))
+    half = (Z // 2) * NC
+
+    def lead_step(i, _):
+        relay(Z // 2 + i // NC, i % NC)
+        return 0
+
+    lax.fori_loop(0, ahead, lead_step, 0)
+
     def work_step(i, _):
-        k, j = Z // 2 + i // NC, i % NC
-        relay(k, j)
-
-        @pl.when(k == last)
+        j = i % NC
+        mine = Z // 2 + i // NC == last
+
+        @pl.when(mine)
+        def _():
+            near(j)
+
+        @pl.when(i + ahead < Z * NC - half)
+        def _():
+            relay(Z // 2 + (i + ahead) // NC, (i + ahead) % NC)
+
+        @pl.when(mine)
         def _():
             chunk(j)
         return 0
 
-    lax.fori_loop(0, (Z - Z // 2) * NC, work_step, 0)
+    lax.fori_loop(0, Z * NC - half, work_step, 0)
 
     for i in range(RT):
         block = row_acc[i * LANES:(i + 1) * LANES, :].T
@@ -475,14 +515,15 @@
     hbm = pl.BlockSpec(memory_space=pl.ANY)
     dma = pltpu.SemaphoreType.DMA
     buf = pl.pallas_call(
-        functools.partial(gather_kernel, MP, DP, W, BM, min(4, NC)),
+        functools.partial(gather_kernel, MP, DP, W, BM, min(3, NC)),
         out_shape=pltpu.VMEM((height, C), F32),
         in_specs=[hbm, hbm, hbm, vmem, vmem],
         out_specs=vmem,
         scratch_shapes=[
             pltpu.VMEM((T * DP, R), jnp.bfloat16),
-            pltpu.VMEM((R, T * DP), jnp.bfloat16),
-            pltpu.VMEM((T * DP, C), jnp.bfloat16),
+            pltpu.VMEM((R, T * (DP - 2)), jnp.bfloat16),
+            pltpu.VMEM((R, 2 * T), jnp.bfloat16),
+            pltpu.VMEM((NC, T * DP, W), jnp.bfloat16),
             pltpu.VMEM((R, LANES), F32),
             pltpu.VMEM((R, LANES), F32),
             pltpu.VMEM((R, LANES), F32),
@@ -491,7 +532,7 @@
             pltpu.VMEM((DP, NC, G, LANES), F32),
             pltpu.VMEM((MP, 2, 8, LANES), F32),
             pltpu.VMEM((DP, 3, 8, LANES), F32),
-            dma((3,)), dma((DP,)), dma((DP,)), dma((DP, MP)),
+            dma((2,)), dma((NC,)), dma((DP,)), dma((DP,)), dma((DP, MP)),
             dma((Z, NC)), dma((Z, NC)), dma((Z, NC)), dma((Z, NC)), dma((Z, NC)),
             dma((MP,)), dma((MP,)), dma((DP, NC)), dma((DP, NC)),
             dma((MP,)), dma((MP,)), dma((DP,)), dma((DP,)),

time: 134 us -> 139 us (1.037)
  Pallas kernels: 133 us -> 138 us
    pallas_call x1, Pallas kernels: 123 us -> 129 us  [on_device(): pl.pallas_call(functools.partial(gather_kernel, MP, DP, W, BM, min(3, NC)...]
where the time goes in v3:
time: 139 us
  Pallas kernels  138 us (99%)
    pallas_call x1, Pallas kernels, on_device(): pl.pallas_call(functools.partial(gather_kernel, MP, DP, W, BM, min(3, NC)...  129 us
    pallas_call x1, Pallas kernels, on_device(): pl.pallas_call(functools.partial(apply_kernel, R, C, BR, SLOTS), out_shap...  9.42 us

profile of v3, /device:TPU:0, one launch (start us, length us, event | category | flops | bytes accessed | tf_op | source)
XLA Modules:
  0.0 138.8 jit_solution(8458502482228786193)
XLA Ops:
  0.6 128.7 %gather_contract.1.buf = f32[2104,4096]{1,0:T(8,128)S(1)} custom-call(bf16[160,8192]{1,0:T(8,128)(2,1)} %x_ref.1, bf16[160,4096]{1,0:T(8,128)(2,1)} %cot_ref.1, f32[1024,4096]{1,0:T(8,128)} %w_ref.1, f32[8,128]{1,0:T(8,128)} %bitcast.5, f32[32,128]{1,0:T(8,128)} %bitcast.4), custom_call_target="tpu_custom_call" | custom-call | flops 10737418240 | bytes 16777216 | tf_op jit(solution)/shard_map/gather_contract/pallas_call | solution.py:517
  129.3 9.4 %apply_update.1 = (f32[1024,4096]{1,0:T(8,128)}, bf16[1024,4096]{1,0:T(8,128)(2,1)}, f32[8,128]{1,0:T(8,128)}, f32[32,128]{1,0:T(8,128)}) custom-call(f32[2104,4096]{1,0:T(8,128)S(1)} %gather_contract.1.buf), custom_call_target="tpu_custom_call" | custom-call | flops 16777216 | bytes 25165824 | tf_op jit(solution)/shard_map/apply_update/pallas_call | solution.py:548

commit v4 on v2

--- a/solution.py
+++ b/solution.py
@@ -196,7 +196,7 @@
         relay(2 + i // NC, i % NC)
         return 0
 
-    lax.fori_loop(0, (Z // 2 - 2) * NC, relay_step, 0)
+    lax.fori_loop(0, (Z - 4) * NC, relay_step, 0)
 
     def rest_step(s, _):
         @pl.when(jnp.logical_and(s != me, taker(s, me) != m))
@@ -250,18 +250,39 @@
 
         lax.fori_loop(0, RT, s_tile, 0)
 
+    half = Z // 2 * 2 * T
+    mine = z // (Z // 2)
+
+    def tokens(h):
+        return pl.ds(pl.multiple_of(h * half, half), half)
+
+    def sib_wait(h, j):
+        def wait(i, _):
+            across_in(h * (Z // 2) + i, j).wait_recv()
+            return 0
+
+        lax.fori_loop(0, Z // 2, wait, 0)
+
+    def first_half(j):
+        sib_wait(mine, j)
+
+        def tile(i, _):
+            rows = pl.ds(pl.multiple_of(i * BM, BM), BM)
+            buf[rows, cols_of(j)] = jnp.dot(
+                a_t[rows, tokens(mine)], call[tokens(mine), cols_of(j)], preferred_element_type=F32
+            )
+            return 0
+
+        lax.fori_loop(0, R // BM, tile, 0)
+
     def chunk(j):
-        def sib_wait(zs, _):
-            @pl.when(zs >= 0)
-            def _():
-                across_in(zs, j).wait_recv()
-            return 0
-
-        lax.fori_loop(0, Z, sib_wait, 0)
+        sib_wait(1 - mine, j)
 
         def tile(i, cacc):
             rows = pl.ds(pl.multiple_of(i * BM, BM), BM)
-            gt = jnp.dot(a_t[rows, :], call[:, cols_of(j)], preferred_element_type=F32)
+            gt = buf[rows, cols_of(j)] + jnp.dot(
+                a_t[rows, tokens(1 - mine)], call[tokens(1 - mine), cols_of(j)], preferred_element_type=F32
+            )
             buf[rows, cols_of(j)] = gt
             sq = gt * gt
             row_acc[rows, :] += sum(sq[:, q * LANES:(q + 1) * LANES] for q in range(G))
@@ -282,18 +303,18 @@
         def _():
             s_part(j - LAG)
 
-    last = jnp.maximum(z, Z - 1 - z)
-
-    def work_step(i, _):
-        k, j = Z // 2 + i // NC, i % NC
-        relay(k, j)
-
-        @pl.when(k == last)
-        def _():
-            chunk(j)
-        return 0
-
-    lax.fori_loop(0, (Z - Z // 2) * NC, work_step, 0)
+    def first_step(j, _):
+        relay(Z - 2, j)
+        first_half(j)
+        return 0
+
+    def last_step(j, _):
+        relay(Z - 1, j)
+        chunk(j)
+        return 0
+
+    lax.fori_loop(0, NC, first_step, 0)
+    lax.fori_loop(0, NC, last_step, 0)
 
     for i in range(RT):
         block = row_acc[i * LANES:(i + 1) * LANES, :].T
@@ -475,7 +496,7 @@
     hbm = pl.BlockSpec(memory_space=pl.ANY)
     dma = pltpu.SemaphoreType.DMA
     buf = pl.pallas_call(
-        functools.partial(gather_kernel, MP, DP, W, BM, min(4, NC)),
+        functools.partial(gather_kernel, MP, DP, W, BM, min(3, NC)),
         out_shape=pltpu.VMEM((height, C), F32),
         in_specs=[hbm, hbm, hbm, vmem, vmem],
         out_specs=vmem,

time: 134 us -> 141 us (1.052)
  Pallas kernels: 133 us -> 140 us
    pallas_call x1, Pallas kernels: 123 us -> 131 us  [on_device(): pl.pallas_call(functools.partial(gather_kernel, MP, DP, W, BM, min(3, NC)...]
where the time goes in v4:
time: 141 us
  Pallas kernels  140 us (99%)
    pallas_call x1, Pallas kernels, on_device(): pl.pallas_call(functools.partial(gather_kernel, MP, DP, W, BM, min(3, NC)...  131 us
    pallas_call x1, Pallas kernels, on_device(): pl.pallas_call(functools.partial(apply_kernel, R, C, BR, SLOTS), out_shap...  9.42 us

profile of v4, /device:TPU:0, one launch (start us, length us, event | category | flops | bytes accessed | tf_op | source)
XLA Modules:
  0.0 140.6 jit_solution(18234209229162802466)
XLA Ops:
  0.6 130.6 %gather_contract.1.buf = f32[2104,4096]{1,0:T(8,128)S(1)} custom-call(bf16[160,8192]{1,0:T(8,128)(2,1)} %x_ref.1, bf16[160,4096]{1,0:T(8,128)(2,1)} %cot_ref.1, f32[1024,4096]{1,0:T(8,128)} %w_ref.1, f32[8,128]{1,0:T(8,128)} %bitcast.5, f32[32,128]{1,0:T(8,128)} %bitcast.4), custom_call_target="tpu_custom_call" | custom-call | flops 10737418240 | bytes 16777216 | tf_op jit(solution)/shard_map/gather_contract/pallas_call | solution.py:498
  131.2 9.4 %apply_update.1 = (f32[1024,4096]{1,0:T(8,128)}, bf16[1024,4096]{1,0:T(8,128)(2,1)}, f32[8,128]{1,0:T(8,128)}, f32[32,128]{1,0:T(8,128)}) custom-call(f32[2104,4096]{1,0:T(8,128)S(1)} %gather_contract.1.buf), custom_call_target="tpu_custom_call" | custom-call | flops 16777216 | bytes 25165824 | tf_op jit(solution)/shard_map/apply_update/pallas_call | solution.py:528

commit v5 on v4

--- a/solution.py
+++ b/solution.py
@@ -17,7 +17,7 @@
 
 
 def gather_kernel(
-    MP, DP, W, BM, LAG,
+    MP, DP, W, BM, LAG, EARLY,
     x_ref, cot_ref, w_ref, rm_ref, cm_ref,
     buf,
     a_raw, a_t, call, row_acc, s_acc, inv_r, n_cols, row_slots, col_slots, s_slots, t_slots,
@@ -250,38 +250,36 @@
 
         lax.fori_loop(0, RT, s_tile, 0)
 
-    half = Z // 2 * 2 * T
-    mine = z // (Z // 2)
-
-    def tokens(h):
-        return pl.ds(pl.multiple_of(h * half, half), half)
-
-    def sib_wait(h, j):
-        def wait(i, _):
-            across_in(h * (Z // 2) + i, j).wait_recv()
-            return 0
-
-        lax.fori_loop(0, Z // 2, wait, 0)
-
-    def first_half(j):
-        sib_wait(mine, j)
+    far_z = jnp.where(z >= Z // 2, 0, Z - 1)
+    late = T * DP - EARLY
+    early_rows = pl.ds(pl.multiple_of(jnp.where(z >= Z // 2, late, 0), late), EARLY)
+    late_rows = pl.ds(pl.multiple_of(jnp.where(z >= Z // 2, 0, EARLY), EARLY), late)
+
+    def first_part(j):
+        def sib_wait(zs, _):
+            @pl.when(zs != far_z)
+            def _():
+                across_in(zs, j).wait_recv()
+            return 0
+
+        lax.fori_loop(0, Z, sib_wait, 0)
 
         def tile(i, _):
             rows = pl.ds(pl.multiple_of(i * BM, BM), BM)
             buf[rows, cols_of(j)] = jnp.dot(
-                a_t[rows, tokens(mine)], call[tokens(mine), cols_of(j)], preferred_element_type=F32
+                a_t[rows, early_rows], call[early_rows, cols_of(j)], preferred_element_type=F32
             )
             return 0
 
         lax.fori_loop(0, R // BM, tile, 0)
 
     def chunk(j):
-        sib_wait(1 - mine, j)
+        across_in(far_z, j).wait_recv()
 
         def tile(i, cacc):
             rows = pl.ds(pl.multiple_of(i * BM, BM), BM)
             gt = buf[rows, cols_of(j)] + jnp.dot(
-                a_t[rows, tokens(1 - mine)], call[tokens(1 - mine), cols_of(j)], preferred_element_type=F32
+                a_t[rows, late_rows], call[late_rows, cols_of(j)], preferred_element_type=F32
             )
             buf[rows, cols_of(j)] = gt
             sq = gt * gt
@@ -305,7 +303,7 @@
 
     def first_step(j, _):
         relay(Z - 2, j)
-        first_half(j)
+        first_part(j)
         return 0
 
     def last_step(j, _):
@@ -492,11 +490,13 @@
     BM = min(512, R)
     RT, CT = R // LANES, C // LANES
     height = extras(R, C)[2] + 16
+    near = T * (DP - 2)
+    early = near // 256 * 256 or near
     vmem = pl.BlockSpec(memory_space=pltpu.VMEM)
     hbm = pl.BlockSpec(memory_space=pl.ANY)
     dma = pltpu.SemaphoreType.DMA
     buf = pl.pallas_call(
-        functools.partial(gather_kernel, MP, DP, W, BM, min(3, NC)),
+        functools.partial(gather_kernel, MP, DP, W, BM, min(4, NC), early),
         out_shape=pltpu.VMEM((height, C), F32),
         in_specs=[hbm, hbm, hbm, vmem, vmem],
         out_specs=vmem,

time: 141 us -> 138 us (0.979)
  Pallas kernels: 140 us -> 137 us
    pallas_call x1, Pallas kernels: 131 us -> 127 us  [on_device(): pl.pallas_call(functools.partial(gather_kernel, MP, DP, W, BM, min(4, NC)...]
where the time goes in v5:
time: 138 us; the launch traced here: 137 us
  Pallas kernels  137 us (99%)
    pallas_call x1, Pallas kernels, on_device(): pl.pallas_call(functools.partial(gather_kernel, MP, DP, W, BM, min(4, NC)...  127 us
    pallas_call x1, Pallas kernels, on_device(): pl.pallas_call(functools.partial(apply_kernel, R, C, BR, SLOTS), out_shap...  9.42 us

profile of v5, /device:TPU:0, one launch (start us, length us, event | category | flops | bytes accessed | tf_op | source)
XLA Modules:
  0.0 137.4 jit_solution(18106752346749540885)
XLA Ops:
  0.6 127.3 %gather_contract.1.buf = f32[2104,4096]{1,0:T(8,128)S(1)} custom-call(bf16[160,8192]{1,0:T(8,128)(2,1)} %x_ref.1, bf16[160,4096]{1,0:T(8,128)(2,1)} %cot_ref.1, f32[1024,4096]{1,0:T(8,128)} %w_ref.1, f32[8,128]{1,0:T(8,128)} %bitcast.5, f32[32,128]{1,0:T(8,128)} %bitcast.4), custom_call_target="tpu_custom_call" | custom-call | flops 10737418240 | bytes 16777216 | tf_op jit(solution)/shard_map/gather_contract/pallas_call | solution.py:498
  127.9 9.4 %apply_update.1 = (f32[1024,4096]{1,0:T(8,128)}, bf16[1024,4096]{1,0:T(8,128)(2,1)}, f32[8,128]{1,0:T(8,128)}, f32[32,128]{1,0:T(8,128)}) custom-call(f32[2104,4096]{1,0:T(8,128)S(1)} %gather_contract.1.buf), custom_call_target="tpu_custom_call" | custom-call | flops 16777216 | bytes 25165824 | tf_op jit(solution)/shard_map/apply_update/pallas_call | solution.py:528
